TPU v7x, 32 devices: a whole 2x2x4 slice. The times are simulated.
32 devices in a mesh: section: 2 (over y), batch: 16 (over z, x, core).
Axes of the slice: x: 2, y: 2, z: 4, core: 2. Of those that a mesh axis runs over, the one named last changes fastest.
Arguments:
- captions: bfloat16 [64, 172, 768], P('batch'), may hold values from -6 to 6
- regions: bfloat16 [16, 36, 768], P('batch'), may hold values from -6 to 6
- image_ids: int32 [64], P('batch'), may hold values from 0 to 15, as said below
- caption_lengths: int32 [64], P('batch'), may hold values from 44 to 172
- cotangent: bfloat16 [64, 208, 768], P('batch'), may hold values from -6 to 6
- query_weight: bfloat16 [2, 768, 768], P('section'), may hold values from -0.21875 to 0.21875
- query_bias: bfloat16 [2, 768], P('section'), may hold values from -2 to 2
- key_weight: bfloat16 [2, 768, 768], P('section'), may hold values from -0.21875 to 0.21875
- value_weight: bfloat16 [2, 768, 768], P('section'), may hold values from -0.21875 to 0.21875
- value_bias: bfloat16 [2, 768], P('section'), may hold values from -2 to 2
- out_weight: bfloat16 [2, 768, 768], P('section'), may hold values from -1.75 to 1.75
- out_bias: bfloat16 [2, 768], P('section'), may hold values from -2 to 2
- norm1_gain: bfloat16 [2, 768], P('section'), may hold values from 0.5 to 1.5
- norm1_bias: bfloat16 [2, 768], P('section'), may hold values from -2 to 2
- up_weight: bfloat16 [2, 768, 3072], P('section'), may hold values from -0.21875 to 0.21875
- up_bias: bfloat16 [2, 3072], P('section'), may hold values from -2 to 2
- down_weight: bfloat16 [2, 3072, 768], P('section'), may hold values from -0.109375 to 0.109375
- down_bias: bfloat16 [2, 768], P('section'), may hold values from -2 to 2
- norm2_gain: bfloat16 [2, 768], P('section'), may hold values from 0.5 to 1.5
- norm2_bias: bfloat16 [2, 768], P('section'), may hold values from -2 to 2
Outputs:
- hidden_states: bfloat16 [2, 64, 208, 768], P('section', 'batch')
- section_grads: bfloat16 [2, 64, 208, 768], P('section', 'batch')
- grad_query_weight: float32 [2, 768, 768], P('section')
- grad_query_bias: float32 [2, 768], P('section')
- grad_key_weight: float32 [2, 768, 768], P('section')
- grad_value_weight: float32 [2, 768, 768], P('section')
- grad_value_bias: float32 [2, 768], P('section')
- grad_out_weight: float32 [2, 768, 768], P('section')
- grad_out_bias: float32 [2, 768], P('section')
- grad_norm1_gain: float32 [2, 768], P('section')
- grad_norm1_bias: float32 [2, 768], P('section')
- grad_up_weight: float32 [2, 768, 3072], P('section')
- grad_up_bias: float32 [2, 3072], P('section')
- grad_down_weight: float32 [2, 3072, 768], P('section')
- grad_down_bias: float32 [2, 768], P('section')
- grad_norm2_gain: float32 [2, 768], P('section')
- grad_norm2_bias: float32 [2, 768], P('section')
Inputs may be any that keep to these rules, and one draw needn't show every extreme that they name: `image_ids`: image m is held at batch index m // 1; the image of item i is held at batch index b = i // 4 or at b - 1 or b + 1 (cyclically), and on every index some item names an image of b - 1 and some item one of b + 1. `caption_lengths`: caption rows at or past this count are padding, masked as keys.
All inputs are finite; a program needn't handle non-finite values.
Results may differ from a plain program's by a relative error of at most 0.029.
Values may be sent and summed in bfloat16 or wider, within the bound.
A program may use at most 320 MiB of HBM per device.

v0:
```python
import functools
import math

import jax
import jax.numpy as jnp
from jax import lax
from jax.experimental import pallas as pl
from jax.experimental.pallas import tpu as pltpu
from jax.sharding import PartitionSpec as P

HEADS = 12
EPSILON = 1e-12
MESH = pl.DeviceIdType.MESH
VMEM_LIMIT = 63 * 1024 * 1024
VMEM_BESIDE = 47 * 1024 * 1024
GROUP = 16
CHUNK_GROUPS = 16
SLOTS = 18
SLOT_GROUPS = 24
LAG = 3
CYCLE = 3
LINE = 4
SPLIT_BITS = 4


def reduce_kernel(
    bits,
    chunks,
    a_hbm,
    b_hbm,
    small_ref,
    whole,
    small_out,
    a_ref,
    b_ref,
    acc,
    recv,
    small_acc,
    small_recv,
    load_sem,
    send_sem,
    recv_sem,
    small_send_sem,
    small_recv_sem,
):
    width = acc.shape[2]
    extra = bits - SPLIT_BITS
    first_gather = SPLIT_BITS + 1 + extra
    stages = 2 * (SPLIT_BITS + 1) + extra
    me = lax.axis_index("batch")
    section = lax.axis_index("section")
    core, side, place = me % 2, (me // 2) % 2, (me // 4) % LINE
    blocks_a = a_hbm.shape[1] // width
    blocks_b = b_hbm.shape[1] // width
    per_block = width // (CHUNK_GROUPS * GROUP)

    def load(source, target, block, base):
        lanes = pl.ds(block * width, width)
        return pltpu.make_async_copy(source.at[:, lanes], target.at[:, lanes], load_sem.at[base + block])

    def load_a(block):
        return load(a_hbm, a_ref, block, 0)

    def load_b(block):
        return load(b_hbm, b_ref, block, blocks_a)

    wide = blocks_a - 3
    first_use = {0: [(load_a, 0), (load_b, 0)]}
    for j in range(1, wide):
        first_use[j] = [(load_a, j)]
    first_use[wide] = [(load_a, wide), (load_b, 1)]
    for j in range(1, wide):
        first_use[wide + j] = [(load_b, 1 + j)]
    first_use[2 * wide] = [(load_a, wide + 1), (load_b, wide + 1)]
    first_use[2 * wide + 1] = [(load_a, wide + 2), (load_b, wide + 2)]
    first_use[2 * wide + 2] = [(load_b, wide + 3)]
    first_use[2 * wide + 3] = [(load_b, wide + 4)]
    for j in range(2 * wide + 4):
        for kind, block in first_use[j]:
            kind(block).start()

    def bit_mate(k):
        bit = (me // 2**k) % 2
        return (section, me + 2**k * (1 - 2 * bit))

    core_mate, side_mate = bit_mate(0), bit_mate(1)
    mates = ((section, me - LINE), (section, me + LINE))
    ring = [(section, me + LINE * ((place + d) % LINE - place)) for d in (LINE - 1, 1)]

    barrier = pltpu.get_barrier_semaphore()
    for peer in [core_mate, side_mate] + ring + [bit_mate(k) for k in range(2, bits)]:
        pl.semaphore_signal(barrier, inc=1, device_id=peer, device_id_type=MESH)
    pl.semaphore_wait(barrier, bits + 2)

    def low_core(c):
        return c * CHUNK_GROUPS + core * 8

    def low_side(c):
        return low_core(c) + side * 4

    def block_start(c, kind, b):
        return low_side(c) + b if kind == 0 else low_core(c) + 2 * b

    def final(c, kind):
        return low_side(c) + place if kind == 0 else low_core(c) + 2 * place + side

    def remote(c, source, start, size, target, spot, index, peer):
        return pltpu.make_async_remote_copy(
            src_ref=source.at[pl.ds(start, size)],
            dst_ref=target.at[lax.rem(c, SLOTS), pl.ds(spot, size)] if target is recv else target.at[pl.ds(start, size)],
            send_sem=send_sem.at[lax.rem(c, SLOTS), index],
            recv_sem=recv_sem.at[lax.rem(c, SLOTS), index],
            device_id=peer,
            device_id_type=MESH,
        )

    def core_copy(c):
        return remote(c, acc, c * CHUNK_GROUPS + (1 - core) * 8, 8, recv, 0, 0, core_mate)

    def side_copy(c, kind):
        if kind == 0:
            return remote(c, acc, low_core(c) + (1 - side) * 4, 4, recv, 8, 1, side_mate)
        return remote(c, acc, low_core(c) + 2 * place + (1 - side), 1, recv, 8, 1, side_mate)

    def line_copy(c, kind, r, d):
        size = 1 + kind
        b = jnp.minimum(3 - r + place, 3) if d == 1 else jnp.maximum(r - 3 + place, 0)
        spot = 12 + 2 * (2 * r + d)
        return remote(c, acc, block_start(c, kind, b), size, recv, spot, 2 + 2 * r + d, mates[d])

    def spread_copy(c, kind, r, d):
        size = 1 + kind
        b = jnp.maximum(place - r, 0) if d == 1 else jnp.minimum(place + r, 3)
        return remote(c, whole, block_start(c, kind, b), size, whole, 0, 8 + 2 * r + d, mates[d])

    def side_back_copy(c, kind):
        if kind == 0:
            return remote(c, whole, low_side(c), 4, whole, 0, 14, side_mate)
        return remote(c, whole, final(c, kind), 1, whole, 0, 14, side_mate)

    def core_back_copy(c):
        return remote(c, whole, low_core(c), 8, whole, 0, 15, core_mate)

    def extra_copy(c, kind, e):
        return remote(c, acc, final(c, kind), 1, recv, 24 + e, 16 + e, bit_mate(SPLIT_BITS + e))

    def add_groups(start, count, c, spot):
        slot = lax.rem(c, SLOTS)
        for g in range(count):
            total = acc[start + g].astype(jnp.float32) + recv[slot, spot + g].astype(jnp.float32)
            acc[start + g] = total.astype(jnp.bfloat16)

    def name_of(kind, s):
        if s == 0:
            return ("core",)
        if s == stages - 1:
            return ("core_back",)
        if s < SPLIT_BITS + 1:
            order = [("side",), ("line", 0), ("line", 1), ("line", 2)]
            order = order if kind == 0 else order[1:] + order[:1]
            return order[s - 1]
        if s < first_gather:
            return ("extra", s - SPLIT_BITS - 1)
        order = [("spread", 0), ("spread", 1), ("spread", 2), ("side_back",)]
        order = order if kind == 0 else order[3:] + order[:3]
        return order[s - first_gather]

    def start_stage(c, kind, s):
        name = name_of(kind, s)
        if s == first_gather:
            whole[final(c, kind)] = acc[final(c, kind)]
        if name[0] == "core":
            core_copy(c).start()
        elif name[0] == "side":
            side_copy(c, kind).start()
        elif name[0] == "line":
            r = name[1]
            pl.when(place <= r)(lambda: line_copy(c, kind, r, 1).start())
            pl.when(place >= 3 - r)(lambda: line_copy(c, kind, r, 0).start())
        elif name[0] == "extra":
            extra_copy(c, kind, name[1]).start()
        elif name[0] == "spread":
            r = name[1]
            pl.when((place >= r) & (place <= 2))(lambda: spread_copy(c, kind, r, 1).start())
            pl.when((place >= 1) & (place <= 3 - r))(lambda: spread_copy(c, kind, r, 0).start())
        elif name[0] == "side_back":
            side_back_copy(c, kind).start()
        else:
            core_back_copy(c).start()

    def finish_stage(c, kind, s):
        name = name_of(kind, s)
        if name[0] == "core":
            core_copy(c).wait()
            add_groups(low_core(c), 8, c, 0)
        elif name[0] == "side":
            side_copy(c, kind).wait()
            if kind == 0:
                add_groups(low_side(c), 4, c, 8)
            else:
                add_groups(final(c, kind), 1, c, 8)
        elif name[0] == "line":
            r = name[1]

            @pl.when(place <= r)
            def _():
                line_copy(c, kind, r, 1).wait_send()

            @pl.when(place >= 3 - r)
            def _():
                line_copy(c, kind, r, 0).wait_send()

            @pl.when((place >= 1) & (place <= r + 1))
            def _():
                line_copy(c, kind, r, 1).wait_recv()
                add_groups(block_start(c, kind, 2 - r + place), 1 + kind, c, 12 + 2 * (2 * r + 1))

            @pl.when((place <= 2) & (place >= 2 - r))
            def _():
                line_copy(c, kind, r, 0).wait_recv()
                add_groups(block_start(c, kind, r - 2 + place), 1 + kind, c, 12 + 2 * (2 * r))

        elif name[0] == "extra":
            extra_copy(c, kind, name[1]).wait()
            add_groups(final(c, kind), 1, c, 24 + name[1])
        elif name[0] == "spread":
            r = name[1]
            pl.when((place >= r) & (place <= 2))(lambda: spread_copy(c, kind, r, 1).wait_send())
            pl.when((place >= 1) & (place <= 3 - r))(lambda: spread_copy(c, kind, r, 0).wait_send())
            pl.when(place >= r + 1)(lambda: spread_copy(c, kind, r, 1).wait_recv())
            pl.when(place <= 2 - r)(lambda: spread_copy(c, kind, r, 0).wait_recv())
        elif name[0] == "side_back":
            side_back_copy(c, kind).wait()
        else:
            core_back_copy(c).wait()

    def small_copy(k):
        return pltpu.make_async_remote_copy(
            src_ref=small_acc.at[k],
            dst_ref=small_recv.at[k],
            send_sem=small_send_sem.at[k],
            recv_sem=small_recv_sem.at[k],
            device_id=bit_mate(k),
            device_id_type=MESH,
        )

    small_acc[0] = small_ref[...]

    def step(t, phase):
        for s in range(stages, 0, -1):
            c = t - LAG * s
            kind = (phase - LAG * s) % CYCLE // 2

            @pl.when((c >= 0) & (c < chunks))
            def _():
                finish_stage(c, kind, s - 1)
                if s < stages:
                    start_stage(c, kind, s)

        for j in range(2 * wide + 4):

            @pl.when(t == per_block * j)
            def _():
                for kind, block in first_use[j]:
                    kind(block).wait()

        @pl.when(t < chunks)
        def _():
            block, part = t // per_block, t % per_block
            a_col = jnp.minimum(block, wide) + jnp.minimum(block // (2 * wide), 1) + jnp.minimum(block // (2 * wide + 1), 1)
            b_col = jnp.maximum(block - wide + 1, 0)
            lines = CHUNK_GROUPS * GROUP
            left = a_ref[:, pl.ds(pl.multiple_of(a_col * width + part * lines, lines), lines)]
            right = b_ref[:, pl.ds(pl.multiple_of(b_col * width, width), width)]
            grad = lax.dot_general(left, right, (((0,), (0,)), ((), ())), preferred_element_type=jnp.float32)
            acc[pl.ds(t * CHUNK_GROUPS, CHUNK_GROUPS)] = grad.astype(jnp.bfloat16).reshape(
                CHUNK_GROUPS, GROUP, width
            )
            core_copy(t).start()

        for k in range(bits + 1):

            @pl.when(t == LAG * k)
            def _():
                if k > 0:
                    small_copy(k - 1).wait()
                    small_acc[k] = small_acc[k - 1] + small_recv[k - 1]
                if k < bits:
                    small_copy(k).start()

    def cycle(n, carry):
        for phase in range(CYCLE):
            step(n * CYCLE + phase, phase)
        return carry

    lax.fori_loop(0, pl.cdiv(chunks + LAG * stages, CYCLE), cycle, 0)
    small_out[...] = small_acc[bits]


def reduced(a_side, b_side, small, count):
    rows = a_side.shape[0]
    width = small.shape[1]
    bits = count.bit_length() - 1
    extra = bits - SPLIT_BITS
    blocks = 2 * (a_side.shape[1] // width - 3) + 4
    chunks = blocks * width // (CHUNK_GROUPS * GROUP)
    groups = chunks * CHUNK_GROUPS
    loads = (a_side.shape[1] + b_side.shape[1]) // width
    return pl.pallas_call(
        functools.partial(reduce_kernel, bits, chunks),
        out_shape=(
            pltpu.VMEM((groups, GROUP, width), jnp.bfloat16),
            jax.ShapeDtypeStruct(small.shape, jnp.float32),
        ),
        in_specs=[
            pl.BlockSpec(memory_space=pl.ANY),
            pl.BlockSpec(memory_space=pl.ANY),
            pl.BlockSpec(memory_space=pltpu.VMEM),
        ],
        out_specs=(pl.BlockSpec(memory_space=pltpu.VMEM), pl.BlockSpec(memory_space=pltpu.VMEM)),
        scratch_shapes=[
            pltpu.VMEM(a_side.shape, jnp.bfloat16),
            pltpu.VMEM(b_side.shape, jnp.bfloat16),
            pltpu.VMEM((groups, GROUP, width), jnp.bfloat16),
            pltpu.VMEM((SLOTS, SLOT_GROUPS + extra, GROUP, width), jnp.bfloat16),
            pltpu.VMEM((bits + 1,) + small.shape, jnp.float32),
            pltpu.VMEM((bits,) + small.shape, jnp.float32),
            pltpu.SemaphoreType.DMA((loads,)),
            pltpu.SemaphoreType.DMA((SLOTS, 16 + extra)),
            pltpu.SemaphoreType.DMA((SLOTS, 16 + extra)),
            pltpu.SemaphoreType.DMA((bits,)),
            pltpu.SemaphoreType.DMA((bits,)),
        ],
        compiler_params=pltpu.CompilerParams(
            collective_id=1, has_side_effects=True, vmem_limit_bytes=VMEM_BESIDE
        ),
        cost_estimate=pl.CostEstimate(
            flops=2 * rows * blocks * width * width, bytes_accessed=80_000_000, transcendentals=0
        ),
    )(a_side, b_side, small)


PIECE = 192
DEPTH = 8


def spread_kernel(sum_ref, small_ref, states_hbm, grads_hbm, *refs):
    width = small_ref.shape[1]
    (o_wq, o_bq, o_wk, o_wv, o_bv, o_wo, o_bo, o_g1, o_s1, o_up, o_bu, o_dn, o_bd, o_g2, o_s2) = refs[2:17]
    states_out, grads_out = refs[:2]
    given, held, out_sem, held_sem = refs[17:]
    wide = o_bu.shape[1] // width
    targets = []
    for j in range(wide):
        targets += [o_dn.at[0, pl.ds(j * width + r, PIECE), :] for r in range(0, width, PIECE)]
    for j in range(wide):
        targets += [o_up.at[0, pl.ds(r, PIECE), pl.ds(j * width, width)] for r in range(0, width, PIECE)]
    for ref in (o_wo, o_wq, o_wk, o_wv):
        targets += [ref.at[0, pl.ds(r, PIECE), :] for r in range(0, width, PIECE)]

    items = states_hbm.shape[1]
    passes = [(states_hbm.at[0, i], states_out.at[0, i]) for i in range(items)]
    passes += [(grads_hbm.at[0, i], grads_out.at[0, i]) for i in range(items)]

    def pass_in(i):
        return pltpu.make_async_copy(passes[i][0], held.at[i], held_sem.at[i])

    def pass_out(i):
        return pltpu.make_async_copy(held.at[i], passes[i][1], held_sem.at[i])

    def store(i):
        return pltpu.make_async_copy(given.at[i % DEPTH], targets[i], out_sem.at[i % DEPTH])

    for i in range(len(passes)):
        pass_in(i).start()
    singles = [o_bq, o_bv, o_bo, o_g1, o_s1, o_bd, o_g2, o_s2]
    for i, ref in enumerate(singles):
        ref[...] = small_ref[pl.ds(i, 1), :]
    for j in range(wide):
        o_bu[:, pl.ds(j * width, width)] = small_ref[pl.ds(len(singles) + j, 1), :]
    for i in range(len(targets)):
        if i >= DEPTH:
            store(i - DEPTH).wait()

        def convert(r, carry):
            block = sum_ref[pl.ds(i * (PIECE // GROUP) + r * 4, 4)].astype(jnp.float32)
            rows = pl.ds(pl.multiple_of(r * 4 * GROUP, 4 * GROUP), 4 * GROUP)
            given[i % DEPTH, rows, :] = block.reshape(4 * GROUP, width)
            return carry

        lax.fori_loop(0, PIECE // (4 * GROUP), convert, 0)
        store(i).start()
        if i < len(passes):
            pass_in(i).wait()
            pass_out(i).start()
    for i in range(len(targets) - DEPTH, len(targets)):
        store(i).wait()
    for i in range(len(passes)):
        pass_out(i).wait()


def spread(sums, small, states, input_grads, params):
    width = small.shape[1]
    anywhere = pl.BlockSpec(memory_space=pl.ANY)
    local = pl.BlockSpec(memory_space=pltpu.VMEM)
    return pl.pallas_call(
        spread_kernel,
        out_shape=(
            jax.ShapeDtypeStruct(states.shape, states.dtype),
            jax.ShapeDtypeStruct(input_grads.shape, input_grads.dtype),
        )
        + tuple(jax.ShapeDtypeStruct(member.shape, jnp.float32) for member in params),
        in_specs=[local, local, anywhere, anywhere],
        out_specs=(anywhere, anywhere)
        + tuple(anywhere if len(member.shape) == 3 else local for member in params),
        scratch_shapes=[
            pltpu.VMEM((DEPTH, PIECE, width), jnp.float32),
            pltpu.VMEM((2 * states.shape[1],) + states.shape[2:], states.dtype),
            pltpu.SemaphoreType.DMA((DEPTH,)),
            pltpu.SemaphoreType.DMA((2 * states.shape[1],)),
        ],
        compiler_params=pltpu.CompilerParams(vmem_limit_bytes=VMEM_BESIDE),
        cost_estimate=pl.CostEstimate(
            flops=12 * width * width, bytes_accessed=80 * width * width, transcendentals=0
        ),
    )(pltpu.with_memory_space_constraint(sums, pltpu.VMEM), small, states, input_grads)


HALF_LOG = -0.5 / math.log(2.0)
BELL_SCALE = 1.0 / math.sqrt(2.0 * math.pi)
SINGLES = ("bq", "bv", "bo", "g1", "s1", "bd", "g2", "s2")


def product(left, right):
    return lax.dot_general(left, right, (((1,), (0,)), ((), ())), preferred_element_type=jnp.float32)


def product_t(left, right):
    return lax.dot_general(left, right, (((1,), (1,)), ((), ())), preferred_element_type=jnp.float32)


def gelu_pair(z):
    cdf = 0.5 * lax.erf(z * (1.0 / math.sqrt(2.0))) + 0.5
    bell = jnp.exp2(z * z * HALF_LOG)
    return z * cdf, z * BELL_SCALE * bell + cdf


def normed(values):
    average = jnp.mean(values, axis=-1, keepdims=True)
    centered = values - average
    inverse = lax.rsqrt(jnp.mean(centered * centered, axis=-1, keepdims=True) + EPSILON)
    return centered * inverse, inverse


def normed_back(grad, normal, inverse):
    first_mean = jnp.mean(grad, axis=-1, keepdims=True)
    second_mean = jnp.mean(grad * normal, axis=-1, keepdims=True)
    return inverse * (grad - first_mean - normal * second_mean)


def layer_kernel(
    ids_ref,
    lengths_ref,
    captions_hbm,
    regions_ref,
    cotangent_hbm,
    wq_hbm,
    bq_ref,
    wk_hbm,
    wv_hbm,
    bv_ref,
    wo_hbm,
    bo_ref,
    g1_ref,
    s1_ref,
    wu_hbm,
    bu_ref,
    wd_hbm,
    bd_ref,
    g2_ref,
    s2_ref,
    states_hbm,
    grads_hbm,
    a_hbm,
    b_hbm,
    small_ref,
    wqkv,
    wo,
    wu,
    wd,
    wqkv_t,
    wo_t,
    wu_t,
    wd_t,
    table,
    hidden,
    upstream,
    query,
    keys,
    values,
    probs,
    context,
    normal1,
    normal2,
    lowered,
    active,
    slope,
    result,
    staged,
    inverses,
    wide1,
    caption_cells,
    weight_sem,
    table_send,
    table_recv,
    fwd_send,
    fwd_recv,
    back_send,
    back_recv,
    out_sem,
):
    items, rows, width = hidden.shape
    held = regions_ref.shape[0]
    cap_rows = captions_hbm.shape[0]
    wide = wu.shape[1] // width
    pairs = HEADS // 2
    pair_width = width // pairs
    head = width // HEADS
    section = lax.axis_index("section")
    batch = lax.axis_index("batch")
    count = lax.axis_size("batch")
    right = (section, lax.rem(batch + 1, count))
    left = (section, lax.rem(batch + count - 1, count))
    other = (1 - section, batch)
    core = lax.rem(batch, 2)

    weight_copies = [
        pltpu.make_async_copy(source.at[0], target, weight_sem.at[n])
        for n, (source, target) in enumerate(
            (
                (wq_hbm, wqkv.at[:, pl.ds(0, width)]),
                (wk_hbm, wqkv.at[:, pl.ds(width, width)]),
                (wv_hbm, wqkv.at[:, pl.ds(2 * width, width)]),
                (wo_hbm, wo),
                (wu_hbm, wu),
                (wd_hbm, wd),
            )
        )
    ]
    for copy in weight_copies[:3]:
        copy.start()
    cotangent_copy = pltpu.make_async_copy(cotangent_hbm, upstream, weight_sem.at[6])

    barrier = pltpu.get_barrier_semaphore()
    for peer in (right, left, other):
        pl.semaphore_signal(barrier, inc=1, device_id=peer, device_id_type=MESH)
    pl.semaphore_wait(barrier, 3)

    def table_copy(n, peer):
        return pltpu.make_async_remote_copy(
            src_ref=regions_ref,
            dst_ref=table.at[pl.ds(2 * n * held, held)],
            send_sem=table_send.at[n],
            recv_sem=table_recv.at[n],
            device_id=peer,
            device_id_type=MESH,
        )

    @pl.when(section == 0)
    def _():
        caption_copy = pltpu.make_async_copy(captions_hbm, caption_cells, weight_sem.at[7])
        caption_copy.start()
        table_copy(0, right).start()
        table_copy(1, left).start()
        table[pl.ds(held, held)] = regions_ref[...]
        table_copy(0, right).wait()
        table_copy(1, left).wait()
        caption_copy.wait()

    for copy in weight_copies[3:]:
        copy.start()

    @pl.when(section == 1)
    def _():
        cotangent_copy.start()

    def forward_copy(i):
        return pltpu.make_async_remote_copy(
            src_ref=result.at[i],
            dst_ref=hidden.at[i],
            send_sem=fwd_send.at[i],
            recv_sem=fwd_recv.at[i],
            device_id=other,
            device_id_type=MESH,
        )

    def back_copy(i):
        return pltpu.make_async_remote_copy(
            src_ref=result.at[i],
            dst_ref=upstream.at[i],
            send_sem=back_send.at[i],
            recv_sem=back_recv.at[i],
            device_id=other,
            device_id_type=MESH,
        )

    def save(i, n):
        at = pl.ds(pl.multiple_of(i * rows, rows), rows)
        first = wide * width
        turn = lax.rem(i, 2)
        if n == 0:
            source, target = active.at[turn], a_hbm.at[at, pl.ds(0, first)]
        elif n == 1:
            source, target = lowered.at[turn], a_hbm.at[at, pl.ds(first, width)]
        elif n == 2:
            source, target = context.at[turn], a_hbm.at[at, pl.ds(first + width, width)]
        elif n == 3:
            source, target = hidden.at[i], a_hbm.at[at, pl.ds(first + 2 * width, width)]
        else:
            source, target = result.at[i], states_hbm.at[0, i]
        return pltpu.make_async_copy(source, target, out_sem.at[i, n])

    def staged_save(i):
        at = pl.ds(pl.multiple_of(i * rows, rows), rows)
        lanes = pl.ds((1 + wide) * width, 4 * width)
        return pltpu.make_async_copy(
            staged.at[lax.rem(i, 2), :, lanes], b_hbm.at[at, lanes], out_sem.at[i, 5]
        )

    def early_save(i):
        at = pl.ds(pl.multiple_of(i * rows, rows), rows)
        lanes = pl.ds(0, (1 + wide) * width)
        return pltpu.make_async_copy(
            staged.at[lax.rem(i, 2), :, lanes], b_hbm.at[at, lanes], out_sem.at[i, 7]
        )

    def grad_save(i):
        return pltpu.make_async_copy(result.at[i], grads_hbm.at[0, i], out_sem.at[i, 6])

    def vector(ref, j=0):
        return ref[:, j * width : (j + 1) * width].astype(jnp.float32)

    lane = lax.broadcasted_iota(jnp.int32, (rows, pair_width), 1)

    blocks = [slice(r, r + GROUP) for r in range(0, rows, GROUP)]
    spans = [slice(c, min(c + 128, rows)) for c in range(0, rows, 128)]

    def only(block, h):
        return jnp.where((lane // head) == h, block, jnp.zeros_like(block))

    def assemble(i):
        total = count * held
        spot = jnp.minimum(lax.rem(ids_ref[i] - (batch - 1) * held + total, total), 3 * held - 1)
        for n in range(items):

            @pl.when(i == n)
            def _():
                whole = jnp.concatenate(
                    [caption_cells[:, n, :].astype(jnp.float32), table[spot].astype(jnp.float32)], axis=0
                )
                hidden[n] = whole.astype(jnp.bfloat16)

    def forward(i):
        @pl.when((i == 0) & (section == 0))
        def _():
            for copy in weight_copies[:3]:
                copy.wait()

        turn = lax.rem(i, 2)
        source = hidden[i]
        mixed = product(source, wqkv[...])
        for at in blocks:
            scaled = (mixed[at, :width] + vector(bq_ref)) * (1.0 / math.sqrt(head))
            query[i, at, :] = scaled.astype(jnp.bfloat16)
            keys[i, at, :] = mixed[at, width : 2 * width].astype(jnp.bfloat16)
            values[i, at, :] = (mixed[at, 2 * width :] + vector(bv_ref)).astype(jnp.bfloat16)
        position = lax.broadcasted_iota(jnp.int32, (rows, 1), 0)
        live = (position >= cap_rows) | (position < lengths_ref[i])
        key_bias = jnp.where(live, 0.0, -1000000000.0)

        def wait_rest():
            @pl.when((i == 0) & (section == 0))
            def _():
                for copy in weight_copies[3:]:
                    copy.wait()

        def lanes_of(p):
            return slice(p * pair_width, (p + 1) * pair_width)

        def scored(p):
            k_pair = keys[i, :, lanes_of(p)]
            stacked = jnp.concatenate([only(k_pair, 0), only(k_pair, 1)], axis=0)
            v_turned = values[i, :, lanes_of(p)].astype(jnp.float32).T.astype(jnp.bfloat16)
            return product_t(stacked, query[i, :, lanes_of(p)]), v_turned

        def weighed(p, both):
            for h in range(2):
                for span in spans:
                    scores = both[h * rows : (h + 1) * rows, span] + key_bias
                    expo = jnp.exp(scores - jnp.max(scores, axis=0, keepdims=True))
                    share = pltpu.reciprocal(jnp.sum(expo, axis=0, keepdims=True), approx=True)
                    probs[i, 2 * p + h, :, span] = (expo * share).astype(jnp.bfloat16)

        def mixed_values(p, v_turned):
            return [product(v_turned[h * head : (h + 1) * head], probs[i, 2 * p + h]) for h in range(2)]

        def place_context(p, parts):
            context[turn, :, lanes_of(p)] = jnp.concatenate(parts, axis=0).T.astype(jnp.bfloat16)

        def projected(group):
            lanes = slice(group * 2 * pair_width, (group + 1) * 2 * pair_width)
            return product(context[turn, :, lanes], wo[lanes, :])

        ahead = scored(0)
        parts = None
        attended = None
        for p in range(pairs):
            both, v_turned = ahead
            if p + 1 < pairs:
                ahead = scored(p + 1)
            if parts is not None:
                place_context(p - 1, parts)
            if p in (2, 4):
                if p == 2:
                    wait_rest()
                piece = projected(p // 2 - 1)
                attended = piece if attended is None else attended + piece
            weighed(p, both)
            parts = mixed_values(p, v_turned)
        place_context(pairs - 1, parts)
        attended += projected(pairs // 2 - 1)

        @pl.when((section == 0) & (core == 1) & (i >= 1))
        def _():
            forward_copy(i - 1).start()

        for at in blocks:
            n1, inv1 = normed(hidden[i, at, :].astype(jnp.float32) + attended[at] + vector(bo_ref))
            normal1[i, at, :] = n1.astype(jnp.bfloat16)
            inverses[i, at, 0:1] = inv1
            first = n1 * vector(g1_ref) + vector(s1_ref)
            lowered[turn, at, :] = first.astype(jnp.bfloat16)
            wide1[at, :] = first + vector(bd_ref)
        half = wide * width // 2

        def raised(n):
            return product(lowered[turn], wu[:, n * half : (n + 1) * half])

        def bend(n, z_tile):
            for part in range(0, half, width):
                lanes = slice(n * half + part, n * half + part + width)
                bias = bu_ref[:, lanes].astype(jnp.float32)
                for at in blocks:
                    gelu, slant = gelu_pair(z_tile[at, part : part + width] + bias)
                    active[turn, at, lanes] = gelu.astype(jnp.bfloat16)
                    slope[i, at, lanes] = slant.astype(jnp.bfloat16)

        z_first = raised(0)
        z_second = raised(1)
        bend(0, z_first)
        wide1[...] += product(active[turn, :, :half], wd[:half, :])
        bend(1, z_second)
        lowest = product(active[turn, :, half:], wd[half:, :])
        for at in blocks:
            n2, inv2 = normed(wide1[at, :] + lowest[at])
            normal2[i, at, :] = n2.astype(jnp.bfloat16)
            inverses[i, at, 1:2] = inv2
            result[i, at, :] = (n2 * vector(g2_ref) + vector(s2_ref)).astype(jnp.bfloat16)

    def folded(value):
        return value[: GROUP // 2] + value[GROUP // 2 :]

    def keep_small(row, value):
        small_ref[row : row + 1, :] += jnp.sum(value, axis=0, keepdims=True)

    def single(name, value):
        keep_small(SINGLES.index(name), value)

    def backward(i):
        slot = lax.rem(i, 2)
        base = (2 + wide) * width

        def stage(at, column, value):
            staged[slot, at, column * width : (column + 1) * width] = value

        def norm_step(at, gradient, normal, layer_norm, gain, sums):
            n = normal[i, at, :].astype(jnp.float32)
            d_res = normed_back(gradient * vector(gain), n, inverses[i, at, layer_norm : layer_norm + 1])
            d_low = d_res.astype(jnp.bfloat16)
            terms = [folded(gradient * n), folded(gradient), folded(d_low.astype(jnp.float32))]
            return d_res, d_low, terms if sums is None else [a + b for a, b in zip(sums, terms)]

        sums = None
        for at in blocks:
            gradient = upstream[i, at, :].astype(jnp.float32)
            d_res, d_low, sums = norm_step(at, gradient, normal2, 1, g2_ref, sums)
            wide1[at, :] = d_res
            stage(at, 0, d_low)
        for name, value in zip(("g2", "s2", "bd"), sums):
            single(name, value)
        d_out = staged[slot, :, :width]
        half = wide * width // 2

        def opened_half(n):
            return product(d_out, wd_t[:, n * half : (n + 1) * half])

        def bent_half(n, d_active):
            for part in range(0, half, width):
                j = (n * half + part) // width
                lanes = slice(j * width, (j + 1) * width)
                total = None
                for at in blocks:
                    d_inner = d_active[at, part : part + width] * slope[i, at, lanes].astype(jnp.float32)
                    d_inner = d_inner.astype(jnp.bfloat16)
                    stage(at, 1 + j, d_inner)
                    term = folded(d_inner.astype(jnp.float32))
                    total = term if total is None else total + term
                keep_small(len(SINGLES) + j, total)

        def closed_half(n):
            at = width + n * half
            return product(staged[slot, :, at : at + half], wu_t[n * half : (n + 1) * half, :])

        d_first = opened_half(0)
        d_second = opened_half(1)
        bent_half(0, d_first)
        d_deep = closed_half(0)
        bent_half(1, d_second)
        d_deeper = closed_half(1)
        early_save(i).start()
        sums = None
        for at in blocks:
            d_res, d_low, sums = norm_step(at, wide1[at, :] + d_deep[at] + d_deeper[at], normal1, 0, g1_ref, sums)
            wide1[at, :] = d_res
            stage(at, 1 + wide, d_low)
        for name, value in zip(("g1", "s1", "bo"), sums):
            single(name, value)
        d_att = staged[slot, :, (1 + wide) * width : (2 + wide) * width]
        @pl.when(i == 0)
        def _():
            save(items - 2, 0).wait()
            save(items - 1, 0).wait()

        active[0, :, :width] = product(d_att, wo_t[...]).astype(jnp.bfloat16)

        def lanes_of(p):
            return slice(p * pair_width, (p + 1) * pair_width)

        def place_grad(n, p, block):
            at = base + n * width + p * pair_width
            staged[slot, :, at : at + pair_width] = block.astype(jnp.bfloat16)

        def opened(p):
            v_pair = values[i, :, lanes_of(p)]
            c_pair = active[0, :, lanes_of(p)]
            stacked = jnp.concatenate([only(v_pair, 0), only(v_pair, 1)], axis=0)
            k_turned = keys[i, :, lanes_of(p)].astype(jnp.float32).T.astype(jnp.bfloat16)
            d_value = product(probs[i, 2 * p], only(c_pair, 0))
            d_value += product(probs[i, 2 * p + 1], only(c_pair, 1))
            return product_t(stacked, c_pair), k_turned, d_value

        def score_base(p, h):
            return (2 * (p % 2) + h) * 2 * 128

        def score_grads(p, both):
            for h in range(2):
                for span in spans:
                    prob = probs[i, 2 * p + h, :, span].astype(jnp.float32)
                    d_prob = both[h * rows : (h + 1) * rows, span]
                    drift = jnp.sum(d_prob * prob, axis=0, keepdims=True)
                    at = score_base(p, h)
                    active[1, :, at + span.start : at + span.stop] = (prob * (d_prob - drift)).astype(jnp.bfloat16)
            return [active[1, :, score_base(p, h) : score_base(p, h) + rows] for h in range(2)]

        def closed(p, found, k_turned):
            q_pair = query[i, :, lanes_of(p)]
            d_key = product(found[0], only(q_pair, 0)) + product(found[1], only(q_pair, 1))
            return d_key, [product(k_turned[h * head : (h + 1) * head], found[h]) for h in range(2)]

        def place_grads(p, d_value, d_key, parts):
            place_grad(0, p, jnp.concatenate(parts, axis=0).T * (1.0 / math.sqrt(head)))
            place_grad(1, p, d_key)
            place_grad(2, p, d_value)

        ahead = opened(0)
        waiting = None
        d_source = None

        def source_grad(group):
            found = None
            for n in range(3):
                at = n * width + group * 2 * pair_width
                piece = product(
                    staged[slot, :, base + at : base + at + 2 * pair_width], wqkv_t[at : at + 2 * pair_width, :]
                )
                found = piece if found is None else found + piece
            return found

        for p in range(pairs):
            both, k_turned, d_value = ahead
            if p + 1 < pairs:
                ahead = opened(p + 1)
            if waiting is not None:
                place_grads(*waiting)
            if p in (2, 4):
                piece = source_grad(p // 2 - 1)
                d_source = piece if d_source is None else d_source + piece
            found = score_grads(p, both)
            d_key, parts = closed(p, found, k_turned)
            waiting = (p, d_value, d_key, parts)
        place_grads(*waiting)
        d_source += source_grad(pairs // 2 - 1)
        sums = None
        for at in blocks:
            result[i, at, :] = (wide1[at, :] + d_source[at]).astype(jnp.bfloat16)
            terms = [
                folded(staged[slot, at, base : base + width].astype(jnp.float32)),
                folded(staged[slot, at, base + 2 * width : base + 3 * width].astype(jnp.float32)),
            ]
            sums = terms if sums is None else [a + b for a, b in zip(sums, terms)]
        single("bq", sums[0])
        single("bv", sums[1])

    small_ref[...] = jnp.zeros_like(small_ref)
    side = 256
    unit = lax.broadcasted_iota(jnp.int32, (side, side), 0) == lax.broadcasted_iota(jnp.int32, (side, side), 1)
    unit = jnp.where(unit, 1.0, 0.0).astype(jnp.bfloat16)

    def turn_weights():
        for natural, turned in ((wqkv, wqkv_t), (wo, wo_t), (wu, wu_t), (wd, wd_t)):
            for block in range(0, natural.shape[0], width):

                def one(n, carry):
                    at = pl.ds(pl.multiple_of(n * side, side), side)
                    tall = product_t(unit, natural[block : block + width, at])
                    turned[at, block : block + width] = tall.astype(jnp.bfloat16)
                    return carry

                lax.fori_loop(0, natural.shape[1] // side, one, 0)

    @pl.when(section == 1)
    def _():
        for copy in weight_copies:
            copy.wait()
        turn_weights()

    def forward_step(i, carry):
        @pl.when(section == 0)
        def _():
            assemble(i)

        @pl.when(section == 1)
        def _():
            forward_copy(i).wait_recv()

        @pl.when(i >= 2)
        def _():
            for n in range(3):
                save(i - 2, n).wait()

        forward(i)

        @pl.when((section == 0) & ((core == 0) | (i == items - 1)))
        def _():
            forward_copy(i).start()

        for n in range(5):
            save(i, n).start()
        return carry

    lax.fori_loop(0, items, forward_step, 0)

    @pl.when(section == 0)
    def _():
        turn_weights()

    @pl.when(section == 1)
    def _():
        cotangent_copy.wait()

    def backward_step(i, carry):
        @pl.when(section == 0)
        def _():
            back_copy(i).wait_recv()

        @pl.when(i >= 2)
        def _():
            staged_save(i - 2).wait()
            early_save(i - 2).wait()

        save(i, 4).wait()

        @pl.when(section == 0)
        def _():
            forward_copy(i).wait_send()

        backward(i)

        @pl.when(section == 1)
        def _():
            back_copy(i).start()

        staged_save(i).start()
        grad_save(i).start()
        return carry

    lax.fori_loop(0, items, backward_step, 0)

    def finish(i, carry):
        save(i, 3).wait()
        grad_save(i).wait()

        @pl.when(i >= items - 2)
        def _():
            staged_save(i).wait()
            early_save(i).wait()
            for n in range(1, 3):
                save(i, n).wait()

        @pl.when(section == 1)
        def _():
            back_copy(i).wait_send()

        return carry

    lax.fori_loop(0, items, finish, 0)


def layered(image_ids, caption_lengths, captions, regions, cotangent, stacked):
    items, cap_rows, width = captions.shape
    held, region_rows, _ = regions.shape
    rows = cap_rows + region_rows
    inner = stacked[9].shape[2]
    low = jnp.bfloat16
    wide = inner // width

    def cells(*shape):
        return pltpu.VMEM(shape, low)

    anywhere = pl.BlockSpec(memory_space=pl.ANY)
    local = pl.BlockSpec(memory_space=pltpu.VMEM)
    scalars = pl.BlockSpec(memory_space=pltpu.SMEM)
    return pl.pallas_call(
        layer_kernel,
        out_shape=(
            jax.ShapeDtypeStruct((1, items, rows, width), low),
            jax.ShapeDtypeStruct((1, items, rows, width), low),
            jax.ShapeDtypeStruct((items * rows, (3 + wide) * width), low),
            jax.ShapeDtypeStruct((items * rows, (5 + wide) * width), low),
            jax.ShapeDtypeStruct((GROUP, width), jnp.float32),
        ),
        in_specs=[scalars, scalars, anywhere, local, anywhere]
        + [anywhere if len(member.shape) == 3 else local for member in stacked],
        out_specs=(anywhere, anywhere, anywhere, anywhere, local),
        scratch_shapes=[
            cells(width, 3 * width),
            cells(width, width),
            cells(width, inner),
            cells(inner, width),
            cells(3 * width, width),
            cells(width, width),
            cells(inner, width),
            cells(width, inner),
            cells(3 * held, region_rows, width),
            cells(items, rows, width),
            cells(items, rows, width),
            cells(items, rows, width),
            cells(items, rows, width),
            cells(items, rows, width),
            cells(items, HEADS, rows, rows),
            cells(2, rows, width),
            cells(items, rows, width),
            cells(items, rows, width),
            cells(2, rows, width),
            cells(2, rows, inner),
            cells(items, rows, inner),
            cells(items, rows, width),
            cells(2, rows, (5 + wide) * width),
            pltpu.VMEM((items, rows, 2), jnp.float32),
            pltpu.VMEM((rows, width), jnp.float32),
            cells(cap_rows, items, width),
            pltpu.SemaphoreType.DMA((8,)),
            pltpu.SemaphoreType.DMA((2,)),
            pltpu.SemaphoreType.DMA((2,)),
            pltpu.SemaphoreType.DMA((items,)),
            pltpu.SemaphoreType.DMA((items,)),
            pltpu.SemaphoreType.DMA((items,)),
            pltpu.SemaphoreType.DMA((items,)),
            pltpu.SemaphoreType.DMA((items, 8)),
        ],
        compiler_params=pltpu.CompilerParams(
            collective_id=0, has_side_effects=True, vmem_limit_bytes=VMEM_LIMIT
        ),
        cost_estimate=pl.CostEstimate(
            flops=4 * items * rows * (4 + 2 * wide) * width * width,
            bytes_accessed=60_000_000,
            transcendentals=0,
        ),
    )(image_ids, caption_lengths, captions.transpose(1, 0, 2), regions, cotangent, *stacked)


def body(
    captions,
    regions,
    image_ids,
    caption_lengths,
    cotangent,
    query_weight,
    query_bias,
    key_weight,
    value_weight,
    value_bias,
    out_weight,
    out_bias,
    norm1_gain,
    norm1_bias,
    up_weight,
    up_bias,
    down_weight,
    down_bias,
    norm2_gain,
    norm2_bias,
):
    stacked = (
        query_weight,
        query_bias,
        key_weight,
        value_weight,
        value_bias,
        out_weight,
        out_bias,
        norm1_gain,
        norm1_bias,
        up_weight,
        up_bias,
        down_weight,
        down_bias,
        norm2_gain,
        norm2_bias,
    )
    states, input_grads, a_side, b_side, small = layered(
        image_ids, caption_lengths, captions, regions, cotangent, stacked
    )
    sums, small_sums = reduced(a_side, b_side, small, lax.axis_size("batch"))
    return tuple(spread(sums, small_sums, states, input_grads, stacked))


def solution(mesh):
    placed = (
        P("batch", None, None),
        P("batch", None, None),
        P("batch"),
        P("batch"),
        P("batch", None, None),
        P("section", None, None),
        P("section", None),
        P("section", None, None),
        P("section", None, None),
        P("section", None),
        P("section", None, None),
        P("section", None),
        P("section", None),
        P("section", None),
        P("section", None, None),
        P("section", None),
        P("section", None, None),
        P("section", None),
        P("section", None),
        P("section", None),
    )
    return jax.shard_map(
        body,
        mesh=mesh,
        in_specs=placed,
        out_specs=(
            P("section", "batch", None, None),
            P("section", "batch", None, None),
            P("section", None, None),
            P("section", None),
            P("section", None, None),
            P("section", None, None),
            P("section", None),
            P("section", None, None),
            P("section", None),
            P("section", None),
            P("section", None),
            P("section", None, None),
            P("section", None),
            P("section", None, None),
            P("section", None),
            P("section", None),
            P("section", None),
        ),
        check_vma=False,
    )
```

profile of v0, /device:TPU:0, one launch (start us, length us, event | category | flops | bytes accessed | tf_op | source)
XLA Modules:
  0.0 253.9 jit_solution(9340961500065596708)
XLA Ops:
  0.7 99.1 %shard_map.323 = (bf16[1,4,208,768]{3,2,1,0:T(8,128)(2,1)}, bf16[1,4,208,768]{3,2,1,0:T(8,128)(2,1)}, bf16[832,5376]{1,0:T(8,128)(2,1)}, bf16[832,6912]{1,0:T(8,128)(2,1)}, f32[16,768]{1,0:T(8,128)}) custom-call(s32[4]{0:T(128)} %ids_ref.1, s32[4]{0:T(128)} %lengths_ref.1, bf16[172,4,768]{2,1,0:T(4,128)(2,1)} %bitcast.1, bf16[1,36,768]{2,1,0:T(8,128)(2,1)} %regions_ref.1, ...), custom_call_target="tpu_custom_call" | custom-call | flops 23555211264 | bytes 60000000 | tf_op jit(solution)/shard_map/pallas_call | solution.py:1043
  99.7 141.6 %shard_map.324 = (bf16[576,16,768]{2,1,0:T(8,128)(2,1)S(1)}, f32[16,768]{1,0:T(8,128)}) custom-call(bf16[832,5376]{1,0:T(8,128)(2,1)} %get-tuple-element.24.a_hbm, bf16[832,6912]{1,0:T(8,128)(2,1)} %get-tuple-element.25.b_hbm, f32[16,768]{1,0:T(8,128)} %get-tuple-element.26.small_ref), custom_call_target="tpu_custom_call" | custom-call | flops 11777605632 | bytes 80000000 | tf_op jit(solution)/shard_map/pallas_call | solution.py:309
  241.3 12.5 %shard_map.325 = (bf16[1,4,208,768]{3,2,1,0:T(8,128)(2,1)}, bf16[1,4,208,768]{3,2,1,0:T(8,128)(2,1)}, f32[1,768,768]{2,1,0:T(8,128)}, f32[1,768]{1,0:T(1,128)}, ...) custom-call(bf16[576,16,768]{2,1,0:T(8,128)(2,1)S(1)} %get-tuple-ele, ...), custom_call_target="tpu_custom_call" | custom-call | flops 7077888 | bytes 47185920 | tf_op jit(solution)/shard_map/pallas_call | solution.py:406
where the time goes:
time: 254 us
  Pallas kernels  253 us (100%)
    pallas_call x1, Pallas kernels, reduced(): pl.pallas_call(functools.partial(reduce_kernel, bits, chunks), out_shape=...  142 us
    pallas_call x1, Pallas kernels, layered(): pl.pallas_call(layer_kernel, out_shape=(jax.ShapeDtypeStruct((1, items, r...  99.1 us
    pallas_call x1, Pallas kernels, spread(): pl.pallas_call(spread_kernel, out_shape=(jax.ShapeDtypeStruct(states.shap...  12.5 us

commit v1 on v0

--- a/solution.py
+++ b/solution.py
@@ -18,7 +18,7 @@
 SLOTS = 18
 SLOT_GROUPS = 24
 LAG = 3
-CYCLE = 3
+EARLY = 6
 LINE = 4
 SPLIT_BITS = 4
 
@@ -246,16 +246,20 @@
 
     small_acc[0] = small_ref[...]
 
-    def step(t, phase):
+    def kind_of(c):
+        early = 1 - jnp.minimum(c // EARLY, 1)
+        return early * (c % 2) + (1 - early) * ((c - EARLY + 4) % 4 // 3)
+
+    def step(t, carry):
         for s in range(stages, 0, -1):
             c = t - LAG * s
-            kind = (phase - LAG * s) % CYCLE // 2
-
-            @pl.when((c >= 0) & (c < chunks))
-            def _():
-                finish_stage(c, kind, s - 1)
-                if s < stages:
-                    start_stage(c, kind, s)
+            for kind in range(2):
+
+                @pl.when((c >= 0) & (c < chunks) & (kind_of(c) == kind))
+                def _():
+                    finish_stage(c, kind, s - 1)
+                    if s < stages:
+                        start_stage(c, kind, s)
 
         for j in range(2 * wide + 4):
 
@@ -288,12 +292,9 @@
                 if k < bits:
                     small_copy(k).start()
 
-    def cycle(n, carry):
-        for phase in range(CYCLE):
-            step(n * CYCLE + phase, phase)
         return carry
 
-    lax.fori_loop(0, pl.cdiv(chunks + LAG * stages, CYCLE), cycle, 0)
+    lax.fori_loop(0, chunks + LAG * stages, step, 0)
     small_out[...] = small_acc[bits]
 
 
@@ -340,8 +341,8 @@
     )(a_side, b_side, small)
 
 
-PIECE = 192
-DEPTH = 8
+PIECE = 768
+DEPTH = 4
 
 
 def spread_kernel(sum_ref, small_ref, states_hbm, grads_hbm, *refs):
@@ -909,6 +910,7 @@
             d_key, parts = closed(p, found, k_turned)
             waiting = (p, d_value, d_key, parts)
         place_grads(*waiting)
+        staged_save(i).start()
         d_source += source_grad(pairs // 2 - 1)
         sums = None
         for at in blocks:
@@ -1000,7 +1002,6 @@
         def _():
             back_copy(i).start()
 
-        staged_save(i).start()
         grad_save(i).start()
         return carry
 

time: 254 us -> 254 us (level)
  no operation moved by 1% of the time
where the time goes in v1:
time: 254 us
  Pallas kernels  253 us (100%)
    pallas_call x1, Pallas kernels, reduced(): pl.pallas_call(functools.partial(reduce_kernel, bits, chunks), out_shape=...  142 us
    pallas_call x1, Pallas kernels, layered(): pl.pallas_call(layer_kernel, out_shape=(jax.ShapeDtypeStruct((1, items, r...  98.7 us
    pallas_call x1, Pallas kernels, spread(): pl.pallas_call(spread_kernel, out_shape=(jax.ShapeDtypeStruct(states.shap...  12 us

profile of v1, /device:TPU:0, one launch (start us, length us, event | category | flops | bytes accessed | tf_op | source)
XLA Modules:
  0.0 253.9 jit_solution(13573277026086771608)
XLA Ops:
  0.7 98.7 %shard_map.323 = (bf16[1,4,208,768]{3,2,1,0:T(8,128)(2,1)}, bf16[1,4,208,768]{3,2,1,0:T(8,128)(2,1)}, bf16[832,5376]{1,0:T(8,128)(2,1)}, bf16[832,6912]{1,0:T(8,128)(2,1)}, f32[16,768]{1,0:T(8,128)}) custom-call(s32[4]{0:T(128)} %ids_ref.1, s32[4]{0:T(128)} %lengths_ref.1, bf16[172,4,768]{2,1,0:T(4,128)(2,1)} %bitcast.1, bf16[1,36,768]{2,1,0:T(8,128)(2,1)} %regions_ref.1, ...), custom_call_target="tpu_custom_call" | custom-call | flops 23555211264 | bytes 60000000 | tf_op jit(solution)/shard_map/pallas_call | solution.py:1044
  99.3 142.4 %shard_map.324 = (bf16[576,16,768]{2,1,0:T(8,128)(2,1)S(1)}, f32[16,768]{1,0:T(8,128)}) custom-call(bf16[832,5376]{1,0:T(8,128)(2,1)} %get-tuple-element.24.a_hbm, bf16[832,6912]{1,0:T(8,128)(2,1)} %get-tuple-element.25.b_hbm, f32[16,768]{1,0:T(8,128)} %get-tuple-element.26.small_ref), custom_call_target="tpu_custom_call" | custom-call | flops 11777605632 | bytes 80000000 | tf_op jit(solution)/shard_map/pallas_call | solution.py:310
  241.8 12.0 %shard_map.325 = (bf16[1,4,208,768]{3,2,1,0:T(8,128)(2,1)}, bf16[1,4,208,768]{3,2,1,0:T(8,128)(2,1)}, f32[1,768,768]{2,1,0:T(8,128)}, f32[1,768]{1,0:T(1,128)}, ...) custom-call(bf16[576,16,768]{2,1,0:T(8,128)(2,1)S(1)} %get-tuple-ele, ...), custom_call_target="tpu_custom_call" | custom-call | flops 7077888 | bytes 47185920 | tf_op jit(solution)/shard_map/pallas_call | solution.py:407

commit v2 on v1

--- a/solution.py
+++ b/solution.py
@@ -37,6 +37,8 @@
     recv,
     small_acc,
     small_recv,
+    turned,
+    unit,
     load_sem,
     send_sem,
     recv_sem,
@@ -245,6 +247,9 @@
         )
 
     small_acc[0] = small_ref[...]
+    lines = CHUNK_GROUPS * GROUP
+    same = lax.broadcasted_iota(jnp.int32, (lines, lines), 0) == lax.broadcasted_iota(jnp.int32, (lines, lines), 1)
+    unit[...] = jnp.where(same, 1.0, 0.0).astype(jnp.bfloat16)
 
     def kind_of(c):
         early = 1 - jnp.minimum(c // EARLY, 1)
@@ -276,7 +281,13 @@
             lines = CHUNK_GROUPS * GROUP
             left = a_ref[:, pl.ds(pl.multiple_of(a_col * width + part * lines, lines), lines)]
             right = b_ref[:, pl.ds(pl.multiple_of(b_col * width, width), width)]
-            grad = lax.dot_general(left, right, (((0,), (0,)), ((), ())), preferred_element_type=jnp.float32)
+            fresh = (block <= wide) | (block == 2 * wide) | (block == 2 * wide + 1)
+
+            @pl.when(fresh)
+            def _():
+                turned[part] = product_t(unit[...], left).astype(jnp.bfloat16)
+
+            grad = product(turned[part], right)
             acc[pl.ds(t * CHUNK_GROUPS, CHUNK_GROUPS)] = grad.astype(jnp.bfloat16).reshape(
                 CHUNK_GROUPS, GROUP, width
             )
@@ -326,6 +337,8 @@
             pltpu.VMEM((SLOTS, SLOT_GROUPS + extra, GROUP, width), jnp.bfloat16),
             pltpu.VMEM((bits + 1,) + small.shape, jnp.float32),
             pltpu.VMEM((bits,) + small.shape, jnp.float32),
+            pltpu.VMEM((width // (CHUNK_GROUPS * GROUP), CHUNK_GROUPS * GROUP, rows), jnp.bfloat16),
+            pltpu.VMEM((CHUNK_GROUPS * GROUP, CHUNK_GROUPS * GROUP), jnp.bfloat16),
             pltpu.SemaphoreType.DMA((loads,)),
             pltpu.SemaphoreType.DMA((SLOTS, 16 + extra)),
             pltpu.SemaphoreType.DMA((SLOTS, 16 + extra)),

time: 254 us -> 256 us (level)
  no operation moved by 1% of the time
where the time goes in v2:
time: 256 us
  Pallas kernels  255 us (100%)
    pallas_call x1, Pallas kernels, reduced(): pl.pallas_call(functools.partial(reduce_kernel, bits, chunks), out_shape=...  144 us
    pallas_call x1, Pallas kernels, layered(): pl.pallas_call(layer_kernel, out_shape=(jax.ShapeDtypeStruct((1, items, r...  98.7 us
    pallas_call x1, Pallas kernels, spread(): pl.pallas_call(spread_kernel, out_shape=(jax.ShapeDtypeStruct(states.shap...  12 us

profile of v2, /device:TPU:0, one launch (start us, length us, event | category | flops | bytes accessed | tf_op | source)
XLA Modules:
  0.0 255.8 jit_solution(15689061942024771753)
XLA Ops:
  0.7 98.7 %shard_map.323 = (bf16[1,4,208,768]{3,2,1,0:T(8,128)(2,1)}, bf16[1,4,208,768]{3,2,1,0:T(8,128)(2,1)}, bf16[832,5376]{1,0:T(8,128)(2,1)}, bf16[832,6912]{1,0:T(8,128)(2,1)}, f32[16,768]{1,0:T(8,128)}) custom-call(s32[4]{0:T(128)} %ids_ref.1, s32[4]{0:T(128)} %lengths_ref.1, bf16[172,4,768]{2,1,0:T(4,128)(2,1)} %bitcast.1, bf16[1,36,768]{2,1,0:T(8,128)(2,1)} %regions_ref.1, ...), custom_call_target="tpu_custom_call" | custom-call | flops 23555211264 | bytes 60000000 | tf_op jit(solution)/shard_map/pallas_call | solution.py:1057
  99.3 144.3 %shard_map.324 = (bf16[576,16,768]{2,1,0:T(8,128)(2,1)S(1)}, f32[16,768]{1,0:T(8,128)}) custom-call(bf16[832,5376]{1,0:T(8,128)(2,1)} %get-tuple-element.24.a_hbm, bf16[832,6912]{1,0:T(8,128)(2,1)} %get-tuple-element.25.b_hbm, f32[16,768]{1,0:T(8,128)} %get-tuple-element.26.small_ref), custom_call_target="tpu_custom_call" | custom-call | flops 11777605632 | bytes 80000000 | tf_op jit(solution)/shard_map/pallas_call | solution.py:321
  243.7 12.0 %shard_map.325 = (bf16[1,4,208,768]{3,2,1,0:T(8,128)(2,1)}, bf16[1,4,208,768]{3,2,1,0:T(8,128)(2,1)}, f32[1,768,768]{2,1,0:T(8,128)}, f32[1,768]{1,0:T(1,128)}, ...) custom-call(bf16[576,16,768]{2,1,0:T(8,128)(2,1)S(1)} %get-tuple-ele, ...), custom_call_target="tpu_custom_call" | custom-call | flops 7077888 | bytes 47185920 | tf_op jit(solution)/shard_map/pallas_call | solution.py:420
